TPU v7x, 32 devices: a whole 2x2x4 slice. The times are simulated.
32 devices in a mesh: groups: 2 (over y), dp: 4 (over z), head: 2 (over x), sub: 2 (over core).
Axes of the slice: x: 2, y: 2, z: 4, core: 2. Of those that a mesh axis runs over, the one named last changes fastest.
Arguments:
- queries: bfloat16 [128, 64, 128], P(('groups', 'dp', 'sub'), 'head'), parts along dimension 0, may hold values from -8 to 8
- kv_cache: bfloat16 [8192, 8, 2, 16, 128], P(('groups', 'dp', 'sub'), 'head'), parts along dimension 0, may hold values from -8 to 8
- keep: int32 [128, 48], P(('groups', 'dp', 'sub')), parts along dimension 0, may hold values from 0 to 63, as said below
- lengths: int32 [128], P(('groups', 'dp', 'sub')), parts along dimension 0, may hold values from 384 to 768
- placement: int32 [128, 64], P(('groups', 'dp', 'sub')), parts along dimension 0, may hold values from 0 to 4095, as said below
- positions: int32 [128], P(('groups', 'dp', 'sub')), parts along dimension 0, may hold values from 0 to 4095
Outputs:
- attention: bfloat16 [128, 64, 128], P(('groups', 'dp', 'sub'), 'head'), parts along dimension 0
- log_norm: float32 [128, 64], P(('groups', 'dp', 'sub'), 'head'), parts along dimension 0
There are 2 independent parts, one for each index of `groups`. A program takes and returns all parts, laid end to end along the dimension named above; each array names one. Nothing has to cross between parts.
Inputs may be any that keep to these rules, and one draw needn't show every extreme that they name: `keep`: each row holds distinct block numbers in increasing order. `placement`: every cache row is named once; the 8 requests of one device (aligned groups of 8 rows) have exactly 64 of their blocks in the cache rows of each device.
All inputs are finite; a program needn't handle non-finite values.
Results may differ from a plain program's by a relative error of at most 0.0058.
Values may be sent and summed in bfloat16 or wider, within the bound.
A program may use at most 128 MiB of HBM per device.

v0:
```python
from functools import partial

import jax
import jax.numpy as jnp
from jax import lax
from jax.sharding import PartitionSpec as P


def rotate(values, positions):
    half = values.shape[-1] // 2
    inverse = 1000000.0 ** (-(2.0 * jnp.arange(half, dtype=jnp.float32)) / values.shape[-1])
    angle = positions.astype(jnp.float32)[:, None] * inverse[None, :]
    cosine = jnp.cos(angle)[:, None, :]
    sine = jnp.sin(angle)[:, None, :]
    first = values[..., :half]
    second = values[..., half:]
    return jnp.concatenate(
        [first * cosine - second * sine, second * cosine + first * sine], axis=-1
    )


def select_rows(row_ids, kv_cache):
    pool_dev = kv_cache.shape[0]
    onehot = (row_ids[:, None] == jnp.arange(pool_dev, dtype=jnp.int32)[None, :]).astype(
        jnp.bfloat16
    )
    picked = jnp.dot(onehot, kv_cache.reshape(pool_dev, -1), preferred_element_type=jnp.float32)
    return picked.astype(jnp.bfloat16).reshape((row_ids.shape[0],) + kv_cache.shape[1:])


def block_partial(selected, blocks, counts):
    factor = selected.shape[-1] ** (-0.5)
    scores = (
        jnp.einsum("skgd,sktd->skgt", selected, blocks[:, :, 0], preferred_element_type=jnp.float32)
        * factor
    )
    live = (jnp.arange(blocks.shape[3], dtype=jnp.int32)[None, :] < counts[:, None])[
        :, None, None, :
    ]
    peak = jnp.max(jnp.where(live, scores, -1e30), axis=-1)
    weights = jnp.where(live, jnp.exp(scores - peak[..., None]), 0.0).astype(jnp.bfloat16)
    totals = jnp.sum(weights.astype(jnp.float32), axis=-1)
    outputs = jnp.einsum(
        "skgt,sktd->skgd", weights, blocks[:, :, 1], preferred_element_type=jnp.float32
    )
    return (peak, totals, outputs)


def combine_slots(peak, totals, outputs, request, requests):
    member = request[None, :] == jnp.arange(requests, dtype=jnp.int32)[:, None]
    inside = member[:, :, None, None]
    top = jnp.max(jnp.where(inside, peak[None], -1e30), axis=1)
    scale = jnp.where(inside, jnp.exp(peak[None] - top[:, None]), 0.0)
    norm = jnp.sum(scale * totals[None], axis=1)
    merged = jnp.einsum("rmkg,mkgd->rkgd", scale, outputs, precision=lax.Precision.HIGHEST)
    return (top, norm, merged)


def local(queries, kv_cache, keep, lengths, placement, positions):
    owners = lax.axis_size(("dp", "sub"))
    requests, q_heads, head_dim = queries.shape
    pool_dev, kv_heads, _, block_len, _ = kv_cache.shape
    spread = pool_dev // owners
    group = q_heads // kv_heads
    kept = keep.shape[1]
    rotated = rotate(queries.astype(jnp.float32), positions).astype(jnp.bfloat16)
    rotated = rotated.reshape(requests, kv_heads, group, head_dim)
    cache_rows = jnp.take_along_axis(placement, keep, axis=1)
    live_counts = jnp.clip(
        lengths[:, None] - jnp.arange(kept, dtype=jnp.int32)[None, :] * block_len, 0, block_len
    )
    owner_of = (cache_rows // pool_dev).reshape(-1)
    local_of = (cache_rows % pool_dev).reshape(-1)
    count_of = live_counts.reshape(-1)
    request_of = jnp.repeat(jnp.arange(requests, dtype=jnp.int32), kept)
    live = count_of > 0
    member = (owner_of[:, None] == jnp.arange(owners, dtype=jnp.int32)[None, :]) & live[:, None]
    running = jnp.cumsum(member.astype(jnp.int32), axis=0) - 1
    ranks = jnp.sum(jnp.where(member, running, 0), axis=1)
    target = jnp.where(live, owner_of * spread + ranks, owners * spread)
    send_ids = jnp.full((owners * spread,), -1, jnp.int32).at[target].set(local_of, mode="drop")
    send_meta = (
        jnp.zeros((owners * spread,), jnp.int32)
        .at[target]
        .set(request_of * (block_len + 1) + count_of, mode="drop")
    )
    send_ids = send_ids.reshape(owners, spread)
    send_meta = send_meta.reshape(owners, spread)
    got_ids, got_meta = (
        lax.all_to_all(send_ids, ("dp", "sub"), split_axis=0, concat_axis=0, tiled=True),
        lax.all_to_all(send_meta, ("dp", "sub"), split_axis=0, concat_axis=0, tiled=True),
    )
    everyone = lax.all_gather(rotated, ("dp", "sub"), axis=0, tiled=True)
    picked = select_rows(got_ids.reshape(-1), kv_cache)
    slot_request = got_meta // (block_len + 1)
    slot_count = (got_meta % (block_len + 1)).reshape(-1)
    source = (jnp.arange(owners, dtype=jnp.int32)[:, None] * requests + slot_request).reshape(-1)
    selected = jnp.take(everyone, source, axis=0)
    peak, totals, outputs = block_partial(selected, picked, slot_count)
    peak = peak.reshape((owners, spread) + peak.shape[1:])
    totals = totals.reshape((owners, spread) + totals.shape[1:])
    outputs = outputs.reshape((owners, spread) + outputs.shape[1:])
    per_source = jax.vmap(partial(combine_slots, requests=requests))
    part_top, part_norm, part_merged = per_source(peak, totals, outputs, slot_request)
    back_top, back_norm, back_merged = (
        lax.all_to_all(part_top, ("dp", "sub"), split_axis=0, concat_axis=0, tiled=True),
        lax.all_to_all(part_norm, ("dp", "sub"), split_axis=0, concat_axis=0, tiled=True),
        lax.all_to_all(part_merged, ("dp", "sub"), split_axis=0, concat_axis=0, tiled=True),
    )
    top = jnp.max(back_top, axis=0)
    scale = jnp.exp(back_top - top[None])
    norm = jnp.sum(scale * back_norm, axis=0)
    merged = jnp.sum(scale[..., None] * back_merged, axis=0)
    attention = (merged / norm[..., None]).reshape(requests, q_heads, head_dim).astype(jnp.bfloat16)
    log_norm = (top + jnp.log(norm)).reshape(requests, q_heads)
    return (attention, log_norm)


def solution(mesh):
    in_specs = (
        P(("groups", "dp", "sub"), "head", None),
        P(("groups", "dp", "sub"), "head", None, None, None),
        P(("groups", "dp", "sub"), None),
        P(("groups", "dp", "sub")),
        P(("groups", "dp", "sub"), None),
        P(("groups", "dp", "sub")),
    )
    out_specs = (P(("groups", "dp", "sub"), "head", None), P(("groups", "dp", "sub"), "head"))
    return jax.shard_map(local, mesh=mesh, in_specs=in_specs, out_specs=out_specs, check_vma=False)
```

profile of v0, /device:TPU:0, one launch (start us, length us, event | category | flops | bytes accessed | tf_op | source)
XLA Modules:
  0.0 181.5 jit_solution(4446497079539612899)
XLA Ops:
  0.7 0.7 fusion.27
  1.6 0.7 bitcast_or_fusion
  2.4 2.1 %gather_fusion.1 = s32[384]{0:T(512)S(1)} fusion(s32[8,64]{1,0:T(8,128)S(1)} %copy-done, s32[384]{0:T(512)S(1)} %reshape.429), kind=kCustom, calls=%fused_computation.1 | custom fusion | bytes 6144 | tf_op jit(solution)/shard_map/jit(take_along_axis)/gather | solution.py:68
  4.5 0.7 and_select_fusion.1
  5.6 0.9 reduce-window.6
  6.8 2.9 %scatter_custom_fusion.1 = s32[512]{0:T(512)S(1)} fusion(s32[384]{0:T(512)S(1)} %fusion.33, s32[384]{0:T(512)S(1)} %get-tuple-element.10, s32[]{:T(128)} %constant.93.clone.1), kind=kCustom, calls=%fused_computation.93 | custom fusion | bytes 2052 | tf_op jit(solution)/shard_map/scatter | solution.py:81
  9.7 0.7 all_to_all.23
  10.4 6.3 %all-to-all-start.1 = ((s32[8,1,64]{2,1,0:T(1,128)}), s32[8,1,64]{2,1,0:T(1,128)S(1)}, u32[]{:S(2)}, u32[]{:S(2)}) async-start(s32[8,1,64]{2,1,0:T(1,128)} %all_to_all.23), calls=%async_computation.1 | async-start | bytes 8192 | tf_op jit(solution)/shard_map/all_to_all | solution.py:90
  16.7 0.7 multiply_add_fusion
  17.5 0.9 convert_element_type.27
  19.3 15.2 %all_gather.3 = bf16[64,4,8,128]{3,2,1,0:T(8,128)(2,1)S(1)} all-gather(bf16[8,4,8,128]{3,2,1,0:T(8,128)(2,1)S(1)} %pad_maximum_fusion), channel_id=1, replica_groups=mesh['groups'=2,'dp'=4,'head'=2,'sub'=2] {'dp','sub'}, dimensions={0}, use_global_device_ids=true | all-gather | bytes 589824 | tf_op jit(solution)/shard_map/all_gather | solution.py:93
  34.9 2.9 %scatter_custom_fusion = s32[512]{0:T(512)S(1)} fusion(s32[384]{0:T(512)S(1)} %fusion.33, s32[384]{0:T(512)S(1)} %reshape.439, s32[]{:T(128)} %constant.59.clone.1), kind=kCustom, calls=%fused_computation.97 | custom fusion | bytes 2052 | tf_op jit(solution)/shard_map/scatter | solution.py:85
  37.8 0.7 all_to_all.21
  38.4 4.7 %all-to-all-start = ((s32[8,1,64]{2,1,0:T(1,128)}), s32[8,1,64]{2,1,0:T(1,128)S(1)}, u32[]{:S(2)}, u32[]{:S(2)}) async-start(s32[8,1,64]{2,1,0:T(1,128)} %all_to_all.21), calls=%async_computation | async-start | bytes 8192 | tf_op jit(solution)/shard_map/all_to_all | solution.py:91
  44.4 22.5 %fusion.6 = bf16[64,8,128,128]{3,1,2,0:T(8,128)(2,1)} fusion(bf16[64,8,128,128]{3,2,1,0:T(8,128)(2,1)} %bitcast.70, s32[512]{0:T(512)S(1)} %eq.69), kind=kOutput, calls=%fused_computation.16 | convolution fusion | flops 8598585344 | bytes 33556480 | tf_op jit(solution)/shard_map/dot_general | solution.py:27
  66.9 15.2 %copy.44 = bf16[64,8,128,128]{3,2,1,0:T(8,128)(2,1)} copy(bf16[64,8,128,128]{3,1,2,0:T(8,128)(2,1)} %fusion.6) | data formatting | bytes 33554432
  83.5 3.4 %gather_fusion = bf16[512,4,8,128]{3,2,1,0:T(8,128)(2,1)} fusion(bf16[64,4,8,128]{3,2,1,0:T(8,128)(2,1)S(1)} %all_gather.3, s32[1024]{0:T(1024)S(1)} %pad_clamp_fusion), kind=kCustom, calls=%fused_computation | custom fusion | bytes 8390656 | tf_op jit(solution)/shard_map/jit(_take)/gather | solution.py:98
  86.9 9.1 %select_reduce_fusion = (f32[512,4,8]{2,1,0:T(4,128)S(1)}, f32[512,4,8,16]{3,2,1,0:T(8,128)S(1)}) fusion(pred[512,16]{1,0:T(8,128)(4,1)S(1)} %iota_compare_fusion.2, bf16[512,4,2,16,128]{4,3,2,1,0:T(8,128)(2,1)} %bitcast.56, bf16[512,4,8,128]{3,2,1,0:T(8,128)(2,1)} %gather_fusion, pred[512]{0:T(512)(128)(4,1)S(1)} %compare_and_fusion.1), kind=kOutput, calls=%fused_computation.15 | convolution fusion | flops 69976064 | bytes 13705728 | tf_op jit(solution)/shard_map/skgd,sktd->skgt/dot_general | solution.py:34
  96.1 9.7 %fusion.2 = f32[512,4,8,128]{3,2,1,0:T(8,128)} fusion(bf16[512,4,2,16,128]{4,3,2,1,0:T(8,128)(2,1)} %bitcast.57, f32[512,4,8,16]{3,2,1,0:T(8,128)S(1)} %get-tuple-element.15, f32[512,4,8]{2,1,0:T(4,128)S(1)} %get-tuple-element.14, pred[512,16]{1,0:T(8,128)(4,1)S(1)} %iota_compare_fusion.2), kind=kOutput, calls=%fused_computation.8 | convolution fusion | flops 68157440 | bytes 17899520 | tf_op jit(solution)/shard_map/skgt,sktd->skgd/dot_general | solution.py:43
  105.7 11.6 %convert_reduce_fusion = f32[512,4,8]{2,1,0:T(4,128)S(1)} fusion(f32[512,4,8]{2,1,0:T(4,128)S(1)} %get-tuple-element.14, f32[512,4,8,16]{3,2,1,0:T(8,128)S(1)} %get-tuple-element.15, pred[512,16]{1,0:T(8,128)(4,1)S(1)} %iota_compare_fusion.2), kind=kLoop, calls=%fused_computation.13 | loop fusion | flops 1556480 | bytes 1187840 | tf_op jit(solution)/shard_map/reduce_sum | solution.py:42
  118.1 0.7 reshape.488
  118.8 5.1 %all-to-all-start.2 = ((f32[8,1,256]{2,1,0:T(1,128)}), f32[8,1,256]{2,1,0:T(1,128)S(1)}, u32[]{:S(2)}, u32[]{:S(2)}) async-start(f32[8,1,256]{2,1,0:T(1,128)} %reshape.488), calls=%async_computation.2 | async-start | bytes 16384 | tf_op jit(solution)/shard_map/all_to_all | solution.py:106
  124.2 0.7 multiply_reduce_fusion
  124.9 0.7 reshape.490
  125.6 3.9 %all-to-all-done.2 = f32[8,1,256]{2,1,0:T(1,128)S(1)} async-done(((f32[8,1,256]{2,1,0:T(1,128)}), f32[8,1,256]{2,1,0:T(1,128)S(1)}, u32[]{:S(2)}, u32[]{:S(2)}) %all-to-all-start.2) | async-done | bytes 8224 | tf_op jit(solution)/shard_map/all_to_all | solution.py:106
  129.5 3.6 %all-to-all-start.4 = ((f32[8,1,256]{2,1,0:T(1,128)}), f32[8,1,256]{2,1,0:T(1,128)S(1)}, u32[]{:S(2)}, u32[]{:S(2)}) async-start(f32[8,1,256]{2,1,0:T(1,128)} %reshape.490), calls=%async_computation.4 | async-start | bytes 16384 | tf_op jit(solution)/shard_map/all_to_all | solution.py:107
  133.1 16.0 %fusion.12 = f32[8,8,4,8,128]{4,1,3,2,0:T(8,128)} fusion(f32[8,64,4,8,128]{4,3,2,1,0:T(8,128)} %bitcast.58, f32[8,8,4,8]{1,3,2,0:T(8,128)S(1)} %select_reduce_fusion.1, f32[8,64,4,8]{1,3,2,0:T(8,128)S(1)} %copy.30, pred[8,8,64]{2,1,0:T(8,128)(4,1)S(1)} %iota_compare_fusion.3), kind=kOutput, calls=%fused_computation.20 | convolution fusion | flops 201588736 | bytes 9515008 | tf_op jit(solution)/shard_map/vmap(rmkg,mkgd->rkgd)/dot_general | solution.py:55
  149.1 4.8 %all-to-all-start.3 = ((f32[8,8,4,8,128]{4,1,3,2,0:T(8,128)}), f32[8,8,4,8,128]{4,1,3,2,0:T(8,128)S(1)}, u32[]{:S(2)}, u32[]{:S(2)}) async-start(f32[8,8,4,8,128]{4,1,3,2,0:T(8,128)} %fusion.12), calls=%async_computation.3 | async-start | bytes 2097152 | tf_op jit(solution)/shard_map/all_to_all | solution.py:108
  154.3 0.7 reduce.21
  155.1 0.7 reduce.22
  156.7 23.7 %all-to-all-done.3 = f32[8,8,4,8,128]{4,1,3,2,0:T(8,128)S(1)} async-done(((f32[8,8,4,8,128]{4,1,3,2,0:T(8,128)}), f32[8,8,4,8,128]{4,1,3,2,0:T(8,128)S(1)}, u32[]{:S(2)}, u32[]{:S(2)}) %all-to-all-start.3) | async-done | bytes 1048608 | tf_op jit(solution)/shard_map/all_to_all | solution.py:108
  180.8 0.7 fusion.20
  (63 shorter events, 7.8 us)
Async XLA Ops:
  0.6 1.7 copy-start
  10.4 28.0 %all-to-all-start.1 = ((s32[8,1,64]{2,1,0:T(1,128)}), s32[8,1,64]{2,1,0:T(1,128)S(1)}, u32[]{:S(2)}, u32[]{:S(2)}) async-start(s32[8,1,64]{2,1,0:T(1,128)} %all_to_all.23), calls=%async_computation.1 | async-start | bytes 8192 | tf_op jit(solution)/shard_map/all_to_all | solution.py:90
  38.4 43.7 %all-to-all-start = ((s32[8,1,64]{2,1,0:T(1,128)}), s32[8,1,64]{2,1,0:T(1,128)S(1)}, u32[]{:S(2)}, u32[]{:S(2)}) async-start(s32[8,1,64]{2,1,0:T(1,128)} %all_to_all.21), calls=%async_computation | async-start | bytes 8192 | tf_op jit(solution)/shard_map/all_to_all | solution.py:91
  117.3 64.1 %copy-start.1 = (s32[8,64]{1,0:T(8,128)S(1)}, s32[8,64]{1,0:T(8,128)}, u32[]{:S(2)}) copy-start(s32[8,64]{1,0:T(8,128)} %param.10) | copy-start | bytes 6148
  118.8 10.7 %all-to-all-start.2 = ((f32[8,1,256]{2,1,0:T(1,128)}), f32[8,1,256]{2,1,0:T(1,128)S(1)}, u32[]{:S(2)}, u32[]{:S(2)}) async-start(f32[8,1,256]{2,1,0:T(1,128)} %reshape.488), calls=%async_computation.2 | async-start | bytes 16384 | tf_op jit(solution)/shard_map/all_to_all | solution.py:106
  129.5 19.6 %all-to-all-start.4 = ((f32[8,1,256]{2,1,0:T(1,128)}), f32[8,1,256]{2,1,0:T(1,128)S(1)}, u32[]{:S(2)}, u32[]{:S(2)}) async-start(f32[8,1,256]{2,1,0:T(1,128)} %reshape.490), calls=%async_computation.4 | async-start | bytes 16384 | tf_op jit(solution)/shard_map/all_to_all | solution.py:107
  149.1 31.4 %all-to-all-start.3 = ((f32[8,8,4,8,128]{4,1,3,2,0:T(8,128)}), f32[8,8,4,8,128]{4,1,3,2,0:T(8,128)S(1)}, u32[]{:S(2)}, u32[]{:S(2)}) async-start(f32[8,8,4,8,128]{4,1,3,2,0:T(8,128)} %fusion.12), calls=%async_computation.3 | async-start | bytes 2097152 | tf_op jit(solution)/shard_map/all_to_all | solution.py:108
where the time goes:
time: 182 us; the launch traced here: 181 us
  matrix products  57.2 us (31%)
  local copies, waits for them, and re-layouts  32.9 us (18%)
  waiting for transfers between devices  27.6 us (15%)
  starting transfers between devices  24.5 us (13%)
  other arithmetic  23.1 us (13%)
  blocking collectives  15.2 us (8%)
    all_to_all x1, waiting for transfers between devices, local(): lax.all_to_all(part_merged, ('dp', 'sub'), split_axis=0, concat_axis=0, t...  23.7 us
    dot_general x1, matrix products, select_rows(): jnp.dot(onehot, kv_cache.reshape(pool_dev, -1), preferred_element_type=jn...  22.5 us
    unnamed x9, local copies, waits for them, and re-layouts  16.8 us
    dot_general x1, matrix products, combine_slots(): jnp.einsum('rmkg,mkgd->rkgd', scale, outputs, precision=lax.Precision.HIG...  16 us
    all_gather x1, blocking collectives, local(): everyone = lax.all_gather(rotated, ('dp', 'sub'), axis=0, tiled=True)  15.2 us
    reduce_sum x1, other arithmetic, block_partial(): totals = jnp.sum(weights.astype(jnp.float32), axis=-1)  11.6 us
    dot_general x1, matrix products, block_partial(): jnp.einsum('skgt,sktd->skgd', weights, blocks[:, :, 1], preferred_element...  9.65 us
    dot_general x1, matrix products, block_partial(): jnp.einsum('skgd,sktd->skgt', selected, blocks[:, :, 0], preferred_elemen...  9.14 us
  transfers between devices with their start and end apart: 5, of which 2 were waited for; matrix products, arithmetic and copies ran while one was open for 36% of the time, Pallas kernels for 0%

commit v1 on v0

v1 whole, which is shorter than its diff:
```python
from functools import partial
import math

import jax
import jax.numpy as jnp
import numpy as np
from jax import lax
from jax.experimental import pallas as pl
from jax.experimental.pallas import tpu as pltpu
from jax.sharding import PartitionSpec as P

MESH = pl.DeviceIdType.MESH
DEAD = -1e30
CHUNKS = 8
F32 = jnp.float32
BF16 = jnp.bfloat16
I32 = jnp.int32


def dot_lanes(a, b):
    return lax.dot_general(a, b, (((1,), (1,)), ((), ())), preferred_element_type=F32)


def iota(shape, axis):
    return lax.broadcasted_iota(I32, shape, axis)


def kernel(
    chips, subs, pos_ref, len_ref, freq_ref, q_ref, keep_ref, place_ref, kv_ref,
    att_ref, log_ref,
    kv, qall, meta_send, meta_recv, meta_s, live_of, own, sib_send, sib_recv, z_send, z_recv, zs_send, zs_recv,
    kv_sem, meta_ssem, meta_rsem, smem_sem, q_ssem, q_rsem, relay_ssem, sib_ssem, sib_rsem,
    z_ssem, z_rsem, zs_ssem, zs_rsem,
):
    owners = chips * subs
    requests, q_heads, head_dim = q_ref.shape
    pool, kv_heads, _, block_len, _ = kv_ref.shape
    group = q_heads // kv_heads
    blocks = place_ref.shape[1]
    kept = keep_ref.shape[1]
    spread = pool // owners
    rows_q = requests * group
    half = head_dim // 2
    scale = head_dim ** -0.5 * math.log2(math.e)
    shift = pool.bit_length() - 1
    my_chip = lax.axis_index("dp")
    my_sub = lax.axis_index("sub")
    me = my_chip * subs + my_sub
    other = 1 - my_sub

    def place(o):
        return {"dp": o // subs, "sub": lax.rem(o, subs)}

    def kv_copy(i):
        part = pl.ds(i * (pool // CHUNKS), pool // CHUNKS)
        return pltpu.make_async_copy(kv_ref.at[part], kv.at[part], kv_sem.at[i])

    def meta_copy(o, slot):
        return pltpu.make_async_remote_copy(
            src_ref=meta_send.at[o], dst_ref=meta_recv.at[slot], send_sem=meta_ssem.at[o],
            recv_sem=meta_rsem.at[slot], device_id=place(o), device_id_type=MESH)

    def q_copy(to, slot, ssem):
        return pltpu.make_async_remote_copy(
            src_ref=qall.at[slot], dst_ref=qall.at[slot], send_sem=ssem,
            recv_sem=q_rsem.at[slot], device_id=place(to), device_id_type=MESH)

    def sib_copy(t):
        return pltpu.make_async_remote_copy(
            src_ref=sib_send.at[t], dst_ref=sib_recv.at[t], send_sem=sib_ssem.at[t],
            recv_sem=sib_rsem.at[t], device_id=place(my_chip * subs + other), device_id_type=MESH)

    def z_copies(t, chip, slot):
        to = place(chip * subs + my_sub)
        return (
            pltpu.make_async_remote_copy(
                src_ref=z_send.at[t], dst_ref=z_recv.at[slot], send_sem=z_ssem.at[t],
                recv_sem=z_rsem.at[slot], device_id=to, device_id_type=MESH),
            pltpu.make_async_remote_copy(
                src_ref=zs_send.at[t], dst_ref=zs_recv.at[slot], send_sem=zs_ssem.at[t],
                recv_sem=zs_rsem.at[slot], device_id=to, device_id_type=MESH),
        )

    barrier = pltpu.get_barrier_semaphore()

    @pl.loop(1, owners)
    def _(i):
        pl.semaphore_signal(barrier, inc=1, device_id=place(lax.rem(me + i, owners)), device_id_type=MESH)

    for i in range(CHUNKS):
        kv_copy(i).start()

    row = iota((requests, 1), 0)
    positions = jnp.zeros((requests, 1), F32)
    for r in range(requests):
        positions = jnp.where(row == r, pos_ref[r].astype(F32), positions)
    angle = positions * freq_ref[...]
    cosine, sine = jnp.cos(angle)[:, None, :], jnp.sin(angle)[:, None, :]
    values = q_ref[...].astype(F32)
    first, second = values[..., :half], values[..., half:]
    rotated = jnp.concatenate([first * cosine - second * sine, second * cosine + first * sine], axis=-1)
    for k in range(kv_heads):
        qall[me, k] = rotated[:, k * group:(k + 1) * group, :].reshape(rows_q, head_dim).astype(BF16)

    table = place_ref[...]
    owner_of = lax.shift_right_logical(table, shift)
    local_of = table & (pool - 1)
    low, high = (local_of & 255).astype(F32), lax.shift_right_logical(local_of, 8).astype(F32)
    member = [
        (owner_of[r:r + 1] == iota((owners, blocks), 0)).astype(F32) for r in range(requests)
    ]
    before = (iota((blocks, blocks), 0) < iota((blocks, blocks), 1)).astype(F32).astype(BF16)
    ranks = jnp.dot(jnp.concatenate(member, 0).astype(BF16), before, preferred_element_type=F32)
    base = jnp.zeros((owners, 1), F32)
    fields = jnp.zeros((3 * owners, spread), F32)
    for r in range(requests):
        m = member[r]
        rank = jnp.sum(m * (ranks[r * owners:(r + 1) * owners] + base), axis=0, keepdims=True)
        base = base + jnp.sum(m, axis=1, keepdims=True)
        at = (rank.astype(I32) == iota((spread, blocks), 0)).astype(F32).astype(BF16)
        named = (keep_ref[r:r + 1, :] == iota((blocks, kept), 0)).astype(F32).astype(BF16)
        live = jnp.clip(len_ref[r] - iota((8, kept), 1) * block_len, 0, block_len)
        count = dot_lanes(live.astype(F32).astype(BF16), named)[:1]
        code = count + float(r * (block_len + 1))
        stacked = jnp.concatenate([m * low[r:r + 1], m * high[r:r + 1], m * code], 0)
        fields = fields + dot_lanes(stacked.astype(BF16), at)
    ids = (fields[:owners] + 256.0 * fields[owners:2 * owners]).astype(I32)
    codes = fields[2 * owners:].astype(I32)
    meta_send[...] = jnp.zeros_like(meta_send)
    for o in range(owners):
        meta_send[o, 0:1, 0:spread] = ids[o:o + 1]
        meta_send[o, 1:2, 0:spread] = codes[o:o + 1]
    meta_recv[me] = meta_send[me]

    pl.semaphore_wait(barrier, owners - 1)

    @pl.loop(1, owners)
    def _(i):
        o = lax.rem(me + i, owners)
        meta_copy(o, me).start()

    @pl.loop(1, chips)
    def _(t):
        chip = lax.rem(my_chip + t, chips)
        q_copy(chip * subs + my_sub, me, q_ssem.at[t]).start()

    q_copy(my_chip * subs + other, me, q_ssem.at[0]).start()

    @pl.loop(1, owners)
    def _(i):
        o = lax.rem(me + i, owners)
        meta_copy(o, o).wait_recv()

    to_smem = pltpu.make_async_copy(meta_recv, meta_s, smem_sem)
    to_smem.start()
    keys = spread * block_len
    expand = (lax.shift_right_logical(iota((spread, keys), 1), block_len.bit_length() - 1)
              == iota((spread, keys), 0)).astype(F32).astype(BF16)
    wide = jnp.dot(meta_recv[:, 1, 0:spread].astype(F32).astype(BF16), expand, preferred_element_type=F32)
    request = jnp.floor((wide + 0.5) * (1.0 / (block_len + 1)))
    count = wide - request * (block_len + 1)
    token = (iota((owners, keys), 1) & (block_len - 1)).astype(F32)
    live_of[...] = jnp.where(token < count, request, -1.0)
    to_smem.wait()
    for i in range(CHUNKS):
        kv_copy(i).wait()

    lane = iota((rows_q, head_dim), 1)

    def attend(o, out):
        wanted = live_of[pl.ds(o, 1), :]
        wanted = jnp.broadcast_to(wanted, (group, keys))
        ids = [meta_s[o, 0, j] & (pool - 1) for j in range(spread)]
        stats = jnp.zeros((rows_q, head_dim), F32)
        for k in range(kv_heads):
            key = jnp.concatenate([kv[ids[j], k, 0] for j in range(spread)], 0)
            value = jnp.concatenate([kv[ids[j], k, 1] for j in range(spread)], 0)
            score = dot_lanes(qall[o, k], key)
            score = jnp.concatenate(
                [jnp.where(wanted == float(r), score[r * group:(r + 1) * group], DEAD) for r in range(requests)], 0)
            peak = jnp.max(score, axis=1, keepdims=True)
            weight = jnp.exp2((score - peak) * scale).astype(BF16)
            total = jnp.sum(weight.astype(F32), axis=1, keepdims=True)
            out[k] = jnp.dot(weight, value, preferred_element_type=F32)
            stats = jnp.where(lane == k, peak, stats)
            stats = jnp.where(lane == kv_heads + k, total, stats)
        out[kv_heads] = stats

    def merge(t):
        a, b = own[t, kv_heads], sib_recv[t, kv_heads]
        stats = jnp.zeros((rows_q, head_dim), F32)
        for k in range(kv_heads):
            ma, mb = a[:, k:k + 1], b[:, k:k + 1]
            la, lb = a[:, kv_heads + k:kv_heads + k + 1], b[:, kv_heads + k:kv_heads + k + 1]
            peak = jnp.maximum(ma, mb)
            wa, wb = jnp.exp2((ma - peak) * scale), jnp.exp2((mb - peak) * scale)
            own[t, k] = own[t, k] * wa + sib_recv[t, k] * wb
            stats = jnp.where(lane == k, peak, stats)
            stats = jnp.where(lane == kv_heads + k, la * wa + lb * wb, stats)
        own[t, kv_heads] = stats

    def send_back(t):
        sib_copy(t).wait_recv()
        merge(t)
        for k in range(kv_heads):
            z_send[t, k] = own[t, k].astype(BF16)
        zs_send[t] = jnp.transpose(own[t, kv_heads])[:2 * kv_heads]
        for copy in z_copies(t, lax.rem(my_chip + t, chips), my_chip):
            copy.start()

    @pl.loop(1, chips + 1)
    def _(i):
        t = lax.rem(i, chips)
        chip = lax.rem(my_chip + t, chips)
        mine, sibs = chip * subs + my_sub, chip * subs + other

        @pl.when(t > 0)
        def _():
            q_copy(my_chip * subs + other, mine, relay_ssem.at[t]).wait_recv()
            q_copy(my_chip * subs + other, mine, relay_ssem.at[t]).start()

        attend(mine, own.at[t])
        q_copy(my_chip * subs + other, sibs, relay_ssem.at[t]).wait_recv()
        attend(sibs, sib_send.at[t])
        sib_copy(t).start()

        @pl.when(i > 1)
        def _():
            send_back(i - 1)

    sib_copy(0).wait_recv()
    merge(0)

    @pl.loop(1, chips)
    def _(t):
        chip = lax.rem(my_chip + t, chips)
        for copy in z_copies(t, chip, chip):
            copy.wait_recv()
        pad = jnp.zeros((head_dim - 2 * kv_heads, rows_q), F32)
        b = jnp.transpose(jnp.concatenate([zs_recv[chip], pad], 0))
        a = own[0, kv_heads]
        stats = jnp.zeros((rows_q, head_dim), F32)
        for k in range(kv_heads):
            ma, mb = a[:, k:k + 1], b[:, k:k + 1]
            la, lb = a[:, kv_heads + k:kv_heads + k + 1], b[:, kv_heads + k:kv_heads + k + 1]
            peak = jnp.maximum(ma, mb)
            wa, wb = jnp.exp2((ma - peak) * scale), jnp.exp2((mb - peak) * scale)
            own[0, k] = own[0, k] * wa + z_recv[chip, k].astype(F32) * wb
            stats = jnp.where(lane == k, peak, stats)
            stats = jnp.where(lane == kv_heads + k, la * wa + lb * wb, stats)
        own[0, kv_heads] = stats

    stats = own[0, kv_heads]
    outs = []
    spot = iota((rows_q, q_heads), 1)
    turn = iota((rows_q, q_heads), 0) & (group - 1)
    logs = jnp.zeros((rows_q, q_heads), F32)
    for k in range(kv_heads):
        norm = stats[:, kv_heads + k:kv_heads + k + 1]
        outs.append((own[0, k] / norm).reshape(requests, group, head_dim))
        value = stats[:, k:k + 1] * (head_dim ** -0.5) + jnp.log(norm)
        logs = jnp.where(spot == turn + k * group, value, logs)
    att_ref[...] = jnp.concatenate(outs, 1).astype(BF16)
    log_ref[...] = jnp.sum(logs.reshape(requests, group, q_heads), axis=1)

    @pl.loop(1, owners)
    def _(i):
        meta_copy(lax.rem(me + i, owners), me).wait_send()

    @pl.loop(0, chips)
    def _(t):
        q_copy(my_chip * subs + other, me, q_ssem.at[t]).wait_send()
        sib_copy(t).wait_send()

    @pl.loop(1, chips)
    def _(t):
        chip = lax.rem(my_chip + t, chips)
        q_copy(my_chip * subs + other, chip * subs + my_sub, relay_ssem.at[t]).wait_send()
        for copy in z_copies(t, chip, my_chip):
            copy.wait_send()


def local(queries, kv_cache, keep, lengths, placement, positions):
    chips, subs = lax.axis_size("dp"), lax.axis_size("sub")
    owners = chips * subs
    requests, q_heads, head_dim = queries.shape
    pool, kv_heads, _, block_len, _ = kv_cache.shape
    spread = pool // owners
    group = q_heads // kv_heads
    rows_q = requests * group
    assert subs == 2 and pool & (pool - 1) == 0 and pool <= 65536
    assert requests * (block_len + 1) <= 256 and block_len & (block_len - 1) == 0
    assert 2 * kv_heads <= head_dim and group & (group - 1) == 0 and spread <= 128
    half = head_dim // 2
    freq = jnp.asarray(
        (1000000.0 ** (-(2.0 * np.arange(half, dtype=np.float64)) / head_dim)).astype(np.float32)[None])
    vmem, smem = pl.BlockSpec(memory_space=pltpu.VMEM), pl.BlockSpec(memory_space=pltpu.SMEM)
    dma = pltpu.SemaphoreType.DMA
    part = (chips, kv_heads + 1, rows_q, head_dim)
    return pl.pallas_call(
        partial(kernel, chips, subs),
        out_shape=(
            jax.ShapeDtypeStruct(queries.shape, BF16),
            jax.ShapeDtypeStruct((requests, q_heads), F32),
        ),
        in_specs=[smem, smem, vmem, vmem, vmem, vmem, pl.BlockSpec(memory_space=pl.ANY)],
        out_specs=(vmem, vmem),
        scratch_shapes=[
            pltpu.VMEM(kv_cache.shape, BF16),
            pltpu.VMEM((owners, kv_heads, rows_q, head_dim), BF16),
            pltpu.VMEM((owners, 8, 128), I32),
            pltpu.VMEM((owners, 8, 128), I32),
            pltpu.SMEM((owners, 8, 128), I32),
            pltpu.VMEM((owners, spread * block_len), F32),
            pltpu.VMEM(part, F32),
            pltpu.VMEM(part, F32),
            pltpu.VMEM(part, F32),
            pltpu.VMEM((chips, kv_heads, rows_q, head_dim), BF16),
            pltpu.VMEM((chips, kv_heads, rows_q, head_dim), BF16),
            pltpu.VMEM((chips, 2 * kv_heads, rows_q), F32),
            pltpu.VMEM((chips, 2 * kv_heads, rows_q), F32),
            dma((CHUNKS,)), dma((owners,)), dma((owners,)), dma,
            dma((chips,)), dma((owners,)), dma((chips,)), dma((chips,)), dma((chips,)),
            dma((chips,)), dma((chips,)), dma((chips,)), dma((chips,)),
        ],
        compiler_params=pltpu.CompilerParams(
            collective_id=0, has_side_effects=True, vmem_limit_bytes=48 * 2 ** 20),
        name="paged",
    )(positions, lengths, freq, queries, keep, placement, kv_cache)


def solution(mesh):
    in_specs = (
        P(("groups", "dp", "sub"), "head", None),
        P(("groups", "dp", "sub"), "head", None, None, None),
        P(("groups", "dp", "sub"), None),
        P(("groups", "dp", "sub")),
        P(("groups", "dp", "sub"), None),
        P(("groups", "dp", "sub")),
    )
    out_specs = (P(("groups", "dp", "sub"), "head", None), P(("groups", "dp", "sub"), "head"))
    return jax.shard_map(local, mesh=mesh, in_specs=in_specs, out_specs=out_specs, check_vma=False)
```

time: 182 us -> 37.4 us (0.21)
  matrix products: 57.2 us -> 0 us
  Pallas kernels: 0 us -> 31.1 us
  waiting for transfers between devices: 27.6 us -> 0 us
  local copies, waits for them, and re-layouts: 32.9 us -> 5.39 us
  starting transfers between devices: 24.5 us -> 0 us
  other arithmetic: 23.1 us -> 0 us
  blocking collectives: 15.2 us -> 0 us
    dot_general x4 -> x0, matrix products: 57.2 us -> none  [the longest x1 22.5 us: select_rows(): jnp.dot(onehot, kv_cache.reshape(pool_dev, -1), preferred_element_type=jn...]
    pallas_call x0 -> x1, Pallas kernels: none -> 31.1 us  [local(): pl.pallas_call(partial(kernel, chips, subs), out_shape=(jax.ShapeDtypeStr...]
    all_to_all x5 -> x0, waiting for transfers between devices: 27.6 us -> none  [the longest x1 23.7 us: local(): lax.all_to_all(part_merged, ('dp', 'sub'), split_axis=0, concat_axis=0, t...]
    all_to_all x5 -> x0, starting transfers between devices: 24.5 us -> none  [the longest x1 6.33 us: local(): lax.all_to_all(send_ids, ('dp', 'sub'), split_axis=0, concat_axis=0, tile...]
    all_gather x1 -> x0, blocking collectives: 15.2 us -> none  [local(): everyone = lax.all_gather(rotated, ('dp', 'sub'), axis=0, tiled=True)]
    reduce_sum x5 -> x0, other arithmetic: 12.8 us -> none  [the longest x1 11.6 us: block_partial(): totals = jnp.sum(weights.astype(jnp.float32), axis=-1)]
    unnamed x9 -> x14, local copies, waits for them, and re-layouts: 16.8 us -> 5.39 us
    scatter x2 -> x0, local copies, waits for them, and re-layouts: 5.82 us -> none  [the longest x1 2.91 us: local(): jnp.full((owners * spread,), -1, jnp.int32).at[target]]
  transfers between devices with their start and end apart: 5 -> 0, of which waited for: 2 -> 0; matrix products, arithmetic and copies ran while one was open for 36% -> 0% of each run, Pallas kernels for 0% -> 0%
where the time goes in v1:
time: 37.4 us; the launch traced here: 37.1 us
  Pallas kernels  31.1 us (83%)
  local copies, waits for them, and re-layouts  5.39 us (14%)
  between operations  0.65 us (2%)
    pallas_call x1, Pallas kernels, local(): pl.pallas_call(partial(kernel, chips, subs), out_shape=(jax.ShapeDtypeStr...  31.1 us
    unnamed x14, local copies, waits for them, and re-layouts  5.39 us

profile of v1, /device:TPU:0, one launch (start us, length us, event | category | flops | bytes accessed | tf_op | source)
XLA Modules:
  0.0 37.1 jit_solution(16071460334755656847)
XLA Ops:
  0.6 0.0 copy-start
  0.6 0.8 %copy-done = bf16[8,32,128]{2,1,0:T(8,128)(2,1)S(1)} copy-done((bf16[8,32,128]{2,1,0:T(8,128)(2,1)S(1)}, bf16[8,32,128]{2,1,0:T(8,128)(2,1)}, u32[]{:S(2)}) %copy-start) | copy-done | bytes 65560
  1.5 0.0 copy-start.1
  1.5 0.7 %copy-done.1 = s32[8,48]{1,0:T(8,128)S(1)} copy-done((s32[8,48]{1,0:T(8,128)S(1)}, s32[8,48]{1,0:T(8,128)}, u32[]{:S(2)}) %copy-start.1) | copy-done | bytes 1560
  2.2 0.0 copy-start.2
  2.2 0.7 %copy-done.2 = s32[8,64]{1,0:T(8,128)S(1)} copy-done((s32[8,64]{1,0:T(8,128)S(1)}, s32[8,64]{1,0:T(8,128)}, u32[]{:S(2)}) %copy-start.2) | copy-done | bytes 2072
  2.8 0.0 copy-start.3
  2.8 0.7 %copy-done.3 = s32[8]{0:T(128)S(1)} copy-done((s32[8]{0:T(128)S(1)}, s32[8]{0:T(128)}, u32[]{:S(2)}) %copy-start.3) | copy-done | bytes 56
  3.5 0.0 copy-start.4
  3.5 0.7 %copy-done.4 = s32[8]{0:T(128)S(1)} copy-done((s32[8]{0:T(128)S(1)}, s32[8]{0:T(128)}, u32[]{:S(2)}) %copy-start.4) | copy-done | bytes 56
  4.2 0.0 copy-start.5
  4.2 0.7 %copy-done.5 = f32[1,64]{1,0:T(1,128)S(1)} copy-done((f32[1,64]{1,0:T(1,128)S(1)}, f32[1,64]{1,0:T(1,128)}, u32[]{:S(2)}) %copy-start.5) | copy-done | bytes 280
  4.8 31.1 %paged.1 = (bf16[8,32,128]{2,1,0:T(8,128)(2,1)S(1)}, f32[8,32]{1,0:T(8,128)S(1)}) custom-call(s32[8]{0:T(128)S(1)} %copy-done.3, s32[8]{0:T(128)S(1)} %copy-done.4, f32[1,64]{1,0:T(1,128)S(1)} %copy-done.5, bf16[8,32,128]{2,1,0:T(8,128)(2,1)S(1)} %copy-done, s32[8,48]{1,0:T(8,128)S(1)} %copy-done.1, s32[8,64]{1,0:T(8,128)S(1)} %copy-done.2, ...), custom_call_target="tpu_custom_call" | custom-call | tf_op jit(solution)/shard_map/paged/pallas_call | solution.py:300
  35.9 0.6 %copy.11 = bf16[8,32,128]{2,1,0:T(8,128)(2,1)} copy(bf16[8,32,128]{2,1,0:T(8,128)(2,1)S(1)} %get-tuple-element.4) | data formatting | bytes 131072
  36.5 0.6 %copy.12 = f32[8,32]{1,0:T(8,128)} copy(f32[8,32]{1,0:T(8,128)S(1)} %get-tuple-element.5) | data formatting | bytes 2048
Async XLA Ops:
  0.6 0.8 %copy-start = (bf16[8,32,128]{2,1,0:T(8,128)(2,1)S(1)}, bf16[8,32,128]{2,1,0:T(8,128)(2,1)}, u32[]{:S(2)}) copy-start(bf16[8,32,128]{2,1,0:T(8,128)(2,1)} %q_ref.1) | copy-start | bytes 196612
  1.5 0.7 %copy-start.1 = (s32[8,48]{1,0:T(8,128)S(1)}, s32[8,48]{1,0:T(8,128)}, u32[]{:S(2)}) copy-start(s32[8,48]{1,0:T(8,128)} %keep_ref.1) | copy-start | bytes 4612
  2.2 0.7 %copy-start.2 = (s32[8,64]{1,0:T(8,128)S(1)}, s32[8,64]{1,0:T(8,128)}, u32[]{:S(2)}) copy-start(s32[8,64]{1,0:T(8,128)} %place_ref.1) | copy-start | bytes 6148
  2.8 0.7 %copy-start.3 = (s32[8]{0:T(128)S(1)}, s32[8]{0:T(128)}, u32[]{:S(2)}) copy-start(s32[8]{0:T(128)} %pos_ref.1) | copy-start | bytes 100
  3.5 0.7 %copy-start.4 = (s32[8]{0:T(128)S(1)}, s32[8]{0:T(128)}, u32[]{:S(2)}) copy-start(s32[8]{0:T(128)} %len_ref.1) | copy-start | bytes 100
  4.2 0.7 %copy-start.5 = (f32[1,64]{1,0:T(1,128)S(1)}, f32[1,64]{1,0:T(1,128)}, u32[]{:S(2)}) copy-start(f32[1,64]{1,0:T(1,128)} %constant.2.clone.freq_ref) | copy-start | bytes 772

commit v2 on v1

--- a/solution.py
+++ b/solution.py
@@ -26,9 +26,9 @@
 
 
 def kernel(
-    chips, subs, pos_ref, len_ref, freq_ref, q_ref, keep_ref, place_ref, kv_ref,
+    chips, subs, pos_hbm, len_hbm, q_hbm, keep_hbm, place_hbm, kv_ref,
     att_ref, log_ref,
-    kv, qall, meta_send, meta_recv, meta_s, live_of, own, sib_send, sib_recv, z_send, z_recv, zs_send, zs_recv,
+    pos_ref, len_ref, q_ref, keep_ref, place_ref, in_sem, own_s, own_live, own_sem, kv, qall, meta_send, meta_recv, meta_s, live_of, own, sib_send, sib_recv, z_send, z_recv, zs_send, zs_recv,
     kv_sem, meta_ssem, meta_rsem, smem_sem, q_ssem, q_rsem, relay_ssem, sib_ssem, sib_rsem,
     z_ssem, z_rsem, zs_ssem, zs_rsem,
 ):
@@ -81,6 +81,14 @@
                 recv_sem=zs_rsem.at[slot], device_id=to, device_id_type=MESH),
         )
 
+    inputs = [
+        pltpu.make_async_copy(source, here, in_sem.at[i])
+        for i, (source, here) in enumerate((
+            (place_hbm, place_ref), (keep_hbm, keep_ref), (len_hbm, len_ref), (pos_hbm, pos_ref), (q_hbm, q_ref)))
+    ]
+    for copy in inputs:
+        copy.start()
+
     barrier = pltpu.get_barrier_semaphore()
 
     @pl.loop(1, owners)
@@ -89,12 +97,20 @@
 
     for i in range(CHUNKS):
         kv_copy(i).start()
+
+    for copy in inputs:
+        copy.wait()
 
     row = iota((requests, 1), 0)
     positions = jnp.zeros((requests, 1), F32)
     for r in range(requests):
         positions = jnp.where(row == r, pos_ref[r].astype(F32), positions)
-    angle = positions * freq_ref[...]
+    place_i = iota((1, half), 1)
+    freq = jnp.ones((1, half), F32)
+    for bit in range(half.bit_length() - 1):
+        step = float(np.float32(1000000.0 ** (-2.0 * 2 ** bit / head_dim)))
+        freq = freq * jnp.where((place_i & (1 << bit)) != 0, step, 1.0)
+    angle = positions * freq
     cosine, sine = jnp.cos(angle)[:, None, :], jnp.sin(angle)[:, None, :]
     values = q_ref[...].astype(F32)
     first, second = values[..., :half], values[..., half:]
@@ -132,6 +148,22 @@
         meta_send[o, 1:2, 0:spread] = codes[o:o + 1]
     meta_recv[me] = meta_send[me]
 
+    own_smem = pltpu.make_async_copy(meta_send.at[me], own_s, own_sem)
+    own_smem.start()
+    keys = spread * block_len
+    expand = (lax.shift_right_logical(iota((spread, keys), 1), block_len.bit_length() - 1)
+              == iota((spread, keys), 0)).astype(F32).astype(BF16)
+
+    def live_requests(codes):
+        wide = jnp.dot(codes.astype(F32).astype(BF16), expand, preferred_element_type=F32)
+        request = jnp.floor((wide + 0.5) * (1.0 / (block_len + 1)))
+        count = wide - request * (block_len + 1)
+        token = (iota(wide.shape, 1) & (block_len - 1)).astype(F32)
+        return jnp.where(token < count, request, -1.0)
+
+    own_live[...] = live_requests(jnp.broadcast_to(meta_send[me, 1:2, 0:spread], (8, spread)))
+    own_smem.wait()
+
     pl.semaphore_wait(barrier, owners - 1)
 
     @pl.loop(1, owners)
@@ -139,38 +171,21 @@
         o = lax.rem(me + i, owners)
         meta_copy(o, me).start()
 
+    q_copy(my_chip * subs + other, me, q_ssem.at[0]).start()
+
     @pl.loop(1, chips)
     def _(t):
         chip = lax.rem(my_chip + t, chips)
         q_copy(chip * subs + my_sub, me, q_ssem.at[t]).start()
 
-    q_copy(my_chip * subs + other, me, q_ssem.at[0]).start()
-
-    @pl.loop(1, owners)
-    def _(i):
-        o = lax.rem(me + i, owners)
-        meta_copy(o, o).wait_recv()
-
-    to_smem = pltpu.make_async_copy(meta_recv, meta_s, smem_sem)
-    to_smem.start()
-    keys = spread * block_len
-    expand = (lax.shift_right_logical(iota((spread, keys), 1), block_len.bit_length() - 1)
-              == iota((spread, keys), 0)).astype(F32).astype(BF16)
-    wide = jnp.dot(meta_recv[:, 1, 0:spread].astype(F32).astype(BF16), expand, preferred_element_type=F32)
-    request = jnp.floor((wide + 0.5) * (1.0 / (block_len + 1)))
-    count = wide - request * (block_len + 1)
-    token = (iota((owners, keys), 1) & (block_len - 1)).astype(F32)
-    live_of[...] = jnp.where(token < count, request, -1.0)
-    to_smem.wait()
     for i in range(CHUNKS):
         kv_copy(i).wait()
 
     lane = iota((rows_q, head_dim), 1)
 
-    def attend(o, out):
-        wanted = live_of[pl.ds(o, 1), :]
-        wanted = jnp.broadcast_to(wanted, (group, keys))
-        ids = [meta_s[o, 0, j] & (pool - 1) for j in range(spread)]
+    def attend(o, live, rows, out):
+        wanted = jnp.broadcast_to(live, (group, keys))
+        ids = [rows[0, j] & (pool - 1) for j in range(spread)]
         stats = jnp.zeros((rows_q, head_dim), F32)
         for k in range(kv_heads):
             key = jnp.concatenate([kv[ids[j], k, 0] for j in range(spread)], 0)
@@ -208,32 +223,45 @@
         for copy in z_copies(t, lax.rem(my_chip + t, chips), my_chip):
             copy.start()
 
-    @pl.loop(1, chips + 1)
+    attend(me, own_live[0:1, :], own_s, own.at[0])
+
+    @pl.loop(1, owners)
     def _(i):
-        t = lax.rem(i, chips)
+        o = lax.rem(me + i, owners)
+        meta_copy(o, o).wait_recv()
+
+    to_smem = pltpu.make_async_copy(meta_recv, meta_s, smem_sem)
+    to_smem.start()
+    live_of[...] = live_requests(meta_recv[:, 1, 0:spread])
+    to_smem.wait()
+
+    @pl.loop(0, chips)
+    def _(t):
         chip = lax.rem(my_chip + t, chips)
         mine, sibs = chip * subs + my_sub, chip * subs + other
 
+        @pl.when(t < chips - 1)
+        def _():
+            ahead = lax.rem(my_chip + t + 1, chips) * subs + my_sub
+            relay = q_copy(my_chip * subs + other, ahead, relay_ssem.at[t + 1])
+            relay.wait_recv()
+            relay.start()
+
+        q_copy(my_chip * subs + other, sibs, relay_ssem.at[t]).wait_recv()
+        attend(sibs, live_of[pl.ds(sibs, 1), :], meta_s.at[sibs], sib_send.at[t])
+        sib_copy(t).start()
+
         @pl.when(t > 0)
         def _():
-            q_copy(my_chip * subs + other, mine, relay_ssem.at[t]).wait_recv()
-            q_copy(my_chip * subs + other, mine, relay_ssem.at[t]).start()
-
-        attend(mine, own.at[t])
-        q_copy(my_chip * subs + other, sibs, relay_ssem.at[t]).wait_recv()
-        attend(sibs, sib_send.at[t])
-        sib_copy(t).start()
-
-        @pl.when(i > 1)
-        def _():
-            send_back(i - 1)
+            attend(mine, live_of[pl.ds(mine, 1), :], meta_s.at[mine], own.at[t])
+            send_back(t)
 
     sib_copy(0).wait_recv()
     merge(0)
 
     @pl.loop(1, chips)
     def _(t):
-        chip = lax.rem(my_chip + t, chips)
+        chip = lax.rem(my_chip + chips - t, chips)
         for copy in z_copies(t, chip, chip):
             copy.wait_recv()
         pad = jnp.zeros((head_dim - 2 * kv_heads, rows_q), F32)
@@ -288,13 +316,11 @@
     spread = pool // owners
     group = q_heads // kv_heads
     rows_q = requests * group
+    assert head_dim & (head_dim - 1) == 0
     assert subs == 2 and pool & (pool - 1) == 0 and pool <= 65536
     assert requests * (block_len + 1) <= 256 and block_len & (block_len - 1) == 0
     assert 2 * kv_heads <= head_dim and group & (group - 1) == 0 and spread <= 128
-    half = head_dim // 2
-    freq = jnp.asarray(
-        (1000000.0 ** (-(2.0 * np.arange(half, dtype=np.float64)) / head_dim)).astype(np.float32)[None])
-    vmem, smem = pl.BlockSpec(memory_space=pltpu.VMEM), pl.BlockSpec(memory_space=pltpu.SMEM)
+    vmem, hbm = pl.BlockSpec(memory_space=pltpu.VMEM), pl.BlockSpec(memory_space=pltpu.HBM)
     dma = pltpu.SemaphoreType.DMA
     part = (chips, kv_heads + 1, rows_q, head_dim)
     return pl.pallas_call(
@@ -303,9 +329,18 @@
             jax.ShapeDtypeStruct(queries.shape, BF16),
             jax.ShapeDtypeStruct((requests, q_heads), F32),
         ),
-        in_specs=[smem, smem, vmem, vmem, vmem, vmem, pl.BlockSpec(memory_space=pl.ANY)],
+        in_specs=[hbm] * 6,
         out_specs=(vmem, vmem),
         scratch_shapes=[
+            pltpu.SMEM(positions.shape, I32),
+            pltpu.SMEM(lengths.shape, I32),
+            pltpu.VMEM(queries.shape, BF16),
+            pltpu.VMEM(keep.shape, I32),
+            pltpu.VMEM(placement.shape, I32),
+            dma((5,)),
+            pltpu.SMEM((8, 128), I32),
+            pltpu.VMEM((8, spread * block_len), F32),
+            dma,
             pltpu.VMEM(kv_cache.shape, BF16),
             pltpu.VMEM((owners, kv_heads, rows_q, head_dim), BF16),
             pltpu.VMEM((owners, 8, 128), I32),
@@ -324,9 +359,9 @@
             dma((chips,)), dma((chips,)), dma((chips,)), dma((chips,)),
         ],
         compiler_params=pltpu.CompilerParams(
-            collective_id=0, has_side_effects=True, vmem_limit_bytes=48 * 2 ** 20),
+            collective_id=0, has_side_effects=True, vmem_limit_bytes=62 * 2 ** 20),
         name="paged",
-    )(positions, lengths, freq, queries, keep, placement, kv_cache)
+    )(positions, lengths, queries, keep, placement, kv_cache)
 
 
 def solution(mesh):

time: 37.4 us -> 32.9 us (0.88)
  local copies, waits for them, and re-layouts: 5.39 us -> 2.74 us
  Pallas kernels: 31.1 us -> 29.3 us
    unnamed x14 -> x2, local copies, waits for them, and re-layouts: 5.39 us -> 2.74 us
    pallas_call x1, Pallas kernels: 31.1 us -> 29.3 us  [local(): pl.pallas_call(partial(kernel, chips, subs), out_shape=(jax.ShapeDtypeStr...]
where the time goes in v2:
time: 32.9 us; the launch traced here: 32.7 us
  Pallas kernels  29.3 us (89%)
  local copies, waits for them, and re-layouts  2.74 us (8%)
  between operations  0.64 us (2%)
    pallas_call x1, Pallas kernels, local(): pl.pallas_call(partial(kernel, chips, subs), out_shape=(jax.ShapeDtypeStr...  29.3 us
    unnamed x2, local copies, waits for them, and re-layouts  2.74 us

profile of v2, /device:TPU:0, one launch (start us, length us, event | category | flops | bytes accessed | tf_op | source)
XLA Modules:
  0.0 32.7 jit_solution(17104510408907268133)
XLA Ops:
  0.6 29.3 %paged.1 = (bf16[8,32,128]{2,1,0:T(8,128)(2,1)}, f32[8,32]{1,0:T(8,128)}) custom-call(s32[8]{0:T(128)} %pos_hbm.1, s32[8]{0:T(128)} %len_hbm.1, bf16[8,32,128]{2,1,0:T(8,128)(2,1)} %q_hbm.1, s32[8,48]{1,0:T(8,128)} %keep_hbm.1, s32[8,64]{1,0:T(8,128)} %place_hbm.1, bf16[512,4,2,16,128]{4,3,2,1,0:T(8,128)(2,1)} %kv_ref.1), custom_call_target="tpu_custom_call" | custom-call | tf_op jit(solution)/shard_map/paged/pallas_call | solution.py:326
  30.0 1.5 %copy.10 = bf16[8,32,128]{2,1,0:T(8,128)(2,1)} copy(bf16[8,32,128]{2,1,0:T(8,128)(2,1)} %get-tuple-element.4) | data formatting | bytes 131072
  31.4 1.3 %copy.11 = f32[8,32]{1,0:T(8,128)} copy(f32[8,32]{1,0:T(8,128)} %get-tuple-element.5) | data formatting | bytes 2048

commit v3 on v2

--- a/solution.py
+++ b/solution.py
@@ -187,18 +187,25 @@
         wanted = jnp.broadcast_to(live, (group, keys))
         ids = [rows[0, j] & (pool - 1) for j in range(spread)]
         stats = jnp.zeros((rows_q, head_dim), F32)
+        scores, weights = [], []
         for k in range(kv_heads):
             key = jnp.concatenate([kv[ids[j], k, 0] for j in range(spread)], 0)
-            value = jnp.concatenate([kv[ids[j], k, 1] for j in range(spread)], 0)
-            score = dot_lanes(qall[o, k], key)
+            scores.append(dot_lanes(qall[o, k], key))
+        for k in range(kv_heads):
             score = jnp.concatenate(
-                [jnp.where(wanted == float(r), score[r * group:(r + 1) * group], DEAD) for r in range(requests)], 0)
+                [jnp.where(wanted == float(r), scores[k][r * group:(r + 1) * group], DEAD) for r in range(requests)], 0)
             peak = jnp.max(score, axis=1, keepdims=True)
             weight = jnp.exp2((score - peak) * scale).astype(BF16)
             total = jnp.sum(weight.astype(F32), axis=1, keepdims=True)
-            out[k] = jnp.dot(weight, value, preferred_element_type=F32)
+            weights.append(weight)
             stats = jnp.where(lane == k, peak, stats)
             stats = jnp.where(lane == kv_heads + k, total, stats)
+        parts = []
+        for k in range(kv_heads):
+            value = jnp.concatenate([kv[ids[j], k, 1] for j in range(spread)], 0)
+            parts.append(jnp.dot(weights[k], value, preferred_element_type=F32))
+        for k in range(kv_heads):
+            out[k] = parts[k]
         out[kv_heads] = stats
 
     def merge(t):

time: 32.9 us -> 30 us (0.912)
  Pallas kernels: 29.3 us -> 26.4 us
    pallas_call x1, Pallas kernels: 29.3 us -> 26.4 us  [local(): pl.pallas_call(partial(kernel, chips, subs), out_shape=(jax.ShapeDtypeStr...]
where the time goes in v3:
time: 30 us; the launch traced here: 29.8 us
  Pallas kernels  26.4 us (88%)
  local copies, waits for them, and re-layouts  2.74 us (9%)
  between operations  0.64 us (2%)
    pallas_call x1, Pallas kernels, local(): pl.pallas_call(partial(kernel, chips, subs), out_shape=(jax.ShapeDtypeStr...  26.4 us
    unnamed x2, local copies, waits for them, and re-layouts  2.74 us

profile of v3, /device:TPU:0, one launch (start us, length us, event | category | flops | bytes accessed | tf_op | source)
XLA Modules:
  0.0 29.8 jit_solution(9333885136115492355)
XLA Ops:
  0.6 26.4 %paged.1 = (bf16[8,32,128]{2,1,0:T(8,128)(2,1)}, f32[8,32]{1,0:T(8,128)}) custom-call(s32[8]{0:T(128)} %pos_hbm.1, s32[8]{0:T(128)} %len_hbm.1, bf16[8,32,128]{2,1,0:T(8,128)(2,1)} %q_hbm.1, s32[8,48]{1,0:T(8,128)} %keep_hbm.1, s32[8,64]{1,0:T(8,128)} %place_hbm.1, bf16[512,4,2,16,128]{4,3,2,1,0:T(8,128)(2,1)} %kv_ref.1), custom_call_target="tpu_custom_call" | custom-call | tf_op jit(solution)/shard_map/paged/pallas_call | solution.py:333
  27.1 1.5 %copy.10 = bf16[8,32,128]{2,1,0:T(8,128)(2,1)} copy(bf16[8,32,128]{2,1,0:T(8,128)(2,1)} %get-tuple-element.4) | data formatting | bytes 131072
  28.6 1.3 %copy.11 = f32[8,32]{1,0:T(8,128)} copy(f32[8,32]{1,0:T(8,128)} %get-tuple-element.5) | data formatting | bytes 2048
